TPU v7x, 32 devices: a whole 2x2x4 slice. The times are simulated.
32 devices in a mesh: rows: 8 (over z, x), sub: 4 (over y, core).
Axes of the slice: x: 2, y: 2, z: 4, core: 2. Of those that a mesh axis runs over, the one named last changes fastest.
Arguments:
- documents: bfloat16 [65536, 1024], P(('rows', 'sub')), may hold values from -40 to 40
- centroids: bfloat16 [1024, 1024], replicated, may hold values from -5 to 5
- cluster_mass: float32 [1024], replicated, may hold values from 0.00024414062 to 0.00390625
Outputs:
- new_centroids: bfloat16 [1024, 1024], P('sub')
- cluster_duals: float32 [1024], replicated
All inputs are finite; a program needn't handle non-finite values.
Results may differ from a plain program's by a relative error of at most 0.0038.
Values may be sent and summed in bfloat16 or wider, within the bound.
A program may use at most 64 MiB of HBM per device.

v0:
```python
import math

import jax
import jax.numpy as jnp
from jax import lax
from jax.sharding import PartitionSpec as P

D = 1024
ITERS = 3


TAU = 0.8
TEMP = 4.0


def per_device(documents, centroids, cluster_mass):
    n_rows = lax.axis_size("rows")
    n_sub = lax.axis_size("sub")
    local_docs = documents.shape[0]
    n_clusters = centroids.shape[0]
    scores = lax.dot_general(
        documents, centroids, (((1,), (1,)), ((), ())), preferred_element_type=jnp.float32
    ) * (TEMP / math.sqrt(D))
    loga = -jnp.log(jnp.asarray(local_docs * n_rows * n_sub, jnp.float32))
    duals = jnp.zeros((n_clusters,), jnp.float32)
    for step in range(ITERS):
        lse = jax.nn.logsumexp(scores + duals[None, :], axis=1)
        row_duals = TAU * (loga - lse)
        mass = jnp.exp(row_duals[:, None] + scores)
        column_mass = lax.psum(jnp.sum(mass, axis=0), ("rows", "sub"))
        duals = TAU * (jnp.log(cluster_mass) - jnp.log(column_mass))
    plan = mass.astype(jnp.bfloat16)
    slab = n_clusters // n_sub
    total = lax.psum(
        lax.dot_general(
            plan, documents, (((0,), (0,)), ((), ())), preferred_element_type=jnp.float32
        ),
        "rows",
    )
    own = lax.psum_scatter(total, "sub", scatter_dimension=0, tiled=True)
    own_mass = lax.dynamic_slice_in_dim(column_mass, lax.axis_index("sub") * slab, slab, 0)
    return ((own / own_mass[:, None]).astype(jnp.bfloat16), duals)


def solution(mesh):
    return jax.shard_map(
        per_device,
        mesh=mesh,
        in_specs=(P(("rows", "sub"), None), P(), P()),
        out_specs=(P("sub", None), P()),
        check_vma=False,
    )
```

profile of v0, /device:TPU:0, one launch (start us, length us, event | category | flops | bytes accessed | tf_op | source)
XLA Modules:
  0.0 263.2 jit_solution(6080413968884662193)
XLA Ops:
  7.2 0.0 copy-start
  7.2 0.0 reduce-scatter.2.cloned.1.call-start
  7.2 1.5 copy-done
  8.8 6.4 %fusion.5 = (f32[2048]{0:T(1024)S(1)}, f32[2048,1024]{0,1:T(8,128)S(1)}) fusion(bf16[2048,1024]{1,0:T(8,128)(2,1)} %param.3, bf16[1024,1024]{1,0:T(8,128)(2,1)S(1)} %copy-done), kind=kOutput, calls=%fused_computation.23 | convolution fusion | flops 4299159552 | bytes 14688256 | tf_op jit(solution)/shard_map/dot_general | solution.py:21
  15.1 0.0 copy-start.1
  15.2 0.0 copy-start.3
  15.2 1.2 exponential_reduce_fusion.4
  16.4 2.0 copy-done.1
  18.4 1.2 exponential_reduce_fusion.3
  19.5 42.0 %psum.28 = f32[1024]{0:T(1024)S(1)} all-reduce(f32[1024]{0:T(1024)S(1)} %exponential_reduce_fusion.3), channel_id=1, replica_groups=mesh['rows'=8,'sub'=4] {'rows','sub'}, use_global_device_ids=true, to_apply=%region_3.0 | all-reduce | flops 1024 | bytes 8192 | tf_op jit(solution)/shard_map/psum | solution.py:30
  61.6 0.0 copy-done.3
  61.6 0.0 copy-start.2
  61.6 4.2 %add_reduce_fusion.1 = f32[2048]{0:T(1024)S(1)} fusion(f32[2048,1024]{0,1:T(8,128)} %copy-done.1, f32[1024]{0:T(1024)S(1)} %subtract_multiply_fusion.5), kind=kLoop, calls=%fused_computation.7 | loop fusion | flops 4192256 | bytes 8400896 | tf_op jit(solution)/shard_map/reduce_max | solution.py:27
  65.8 1.6 copy-done.2
  67.3 1.8 exponential_reduce_fusion.2
  69.2 1.2 exponential_reduce_fusion.1
  70.4 40.4 %psum.29 = f32[1024]{0:T(1024)S(1)} all-reduce(f32[1024]{0:T(1024)S(1)} %exponential_reduce_fusion.1), channel_id=1, replica_groups=mesh['rows'=8,'sub'=4] {'rows','sub'}, use_global_device_ids=true, to_apply=%region_7.0 | all-reduce | flops 1024 | bytes 8192 | tf_op jit(solution)/shard_map/psum | solution.py:30
  110.7 0.0 slice-start
  110.8 0.0 copy-start.4
  110.8 4.2 %add_reduce_fusion = f32[2048]{0:T(1024)S(1)} fusion(f32[2048,1024]{0,1:T(8,128)} %copy-done.1, f32[1024]{0:T(1024)S(1)} %subtract_multiply_fusion.4), kind=kLoop, calls=%fused_computation.6 | loop fusion | flops 4192256 | bytes 8400896 | tf_op jit(solution)/shard_map/reduce_max | solution.py:27
  114.9 0.0 slice-start.1
  114.9 4.9 %exponential_reduce_fusion = f32[2048]{0:T(1024)S(1)} fusion(f32[2048,1024]{0,1:T(8,128)} %copy-done.1, f32[2048]{0:T(1024)S(1)} %is-finite_select_fusion, f32[1024]{0:T(1024)S(1)} %subtract_multiply_fusion.4), kind=kLoop, calls=%fused_computation.1 | loop fusion | flops 6289408 | bytes 8409088 | tf_op jit(solution)/shard_map/reduce_sum | solution.py:27
  119.9 0.0 slice-done
  119.9 0.0 copy-done.4
  119.9 0.5 slice-done.1
  120.5 6.1 %fusion.2 = f32[1024,1024]{1,0:T(8,128)} fusion(bf16[2048,1024]{1,0:T(8,128)(2,1)S(1)} %copy-done.4, f32[2048,1024]{0,1:T(8,128)S(1)} %bitcast.4, f32[2048]{0:T(1024)S(1)} %subtract_multiply_fusion), kind=kOutput, calls=%fused_computation.11 | convolution fusion | flops 4299161600 | bytes 16785408 | tf_op jit(solution)/shard_map/dot_general | solution.py:35
  126.6 0.0 reduce-scatter.2.cloned.1.call-update
  126.6 0.0 all-reduce.2.cloned.1.call-start
  126.7 45.3 %reduce-scatter.2.cloned.1.call-done = f32[256,1024]{1,0:T(8,128)} async-done(((f32[1024,1024]{1,0:T(8,128)}), f32[256,1024]{1,0:T(8,128)}) %reduce-scatter.2.cloned.1.call-update) | async-done | bytes 1048592 | tf_op jit(solution)/shard_map/reduce_scatter | solution.py:40
  171.9 0.0 all-reduce.2.cloned.1.call-update
  171.9 4.6 %fusion = f32[1024]{0:T(1024)S(1)} fusion(f32[2048,1024]{0,1:T(8,128)} %copy-done.1, f32[2048]{0:T(1024)S(1)} %subtract_multiply_fusion), kind=kLoop, calls=%fused_computation.8 | loop fusion | flops 4193280 | bytes 8400896 | tf_op jit(solution)/shard_map/reduce_sum | solution.py:30
  176.5 39.6 %psum.31 = f32[1024]{0:T(1024)S(1)} all-reduce(f32[1024]{0:T(1024)S(1)} %fusion), channel_id=1, replica_groups=mesh['rows'=8,'sub'=4] {'rows','sub'}, use_global_device_ids=true, to_apply=%region_13.0 | all-reduce | flops 1024 | bytes 8192 | tf_op jit(solution)/shard_map/psum | solution.py:30
  216.2 0.1 dynamic_slice.3
  216.2 0.6 subtract_multiply_fusion.3
  216.8 37.3 %all-reduce.2.cloned.1.call-done = f32[256,1024]{1,0:T(8,128)} async-done(((f32[256,1024]{1,0:T(8,128)}), f32[256,1024]{1,0:T(8,128)}) %all-reduce.2.cloned.1.call-update) | async-done | bytes 1048592 | tf_op jit(solution)/shard_map/psum | solution.py:34
  254.2 2.2 divide_convert_fusion
  (9 shorter events, 0.1 us)
Async XLA Ops:
  7.2 1.6 copy-start
  7.2 164.7 %reduce-scatter.2.cloned.1.call-start = ((), (), s32[]{:S(2)}) async-start(), calls=%async_computation.1 | async-start | bytes 5242880 | tf_op jit(solution)/shard_map/reduce_scatter | solution.py:40
  15.1 3.2 %copy-start.1 = (f32[2048,1024]{0,1:T(8,128)}, f32[2048,1024]{0,1:T(8,128)S(1)}, u32[]{:S(2)}) copy-start(f32[2048,1024]{0,1:T(8,128)S(1)} %get-tuple-element.3) | copy-start | bytes 25165828
  15.2 46.4 %copy-start.3 = (f32[1024]{0:T(1024)S(1)}, f32[1024]{0:T(1024)}, u32[]{:S(2)}) copy-start(f32[1024]{0:T(1024)} %param.5) | copy-start | bytes 12292
  61.6 5.8 %copy-start.2 = (f32[2048,1024]{0,1:T(8,128)S(1)}, f32[2048,1024]{0,1:T(8,128)}, u32[]{:S(2)}) copy-start(f32[2048,1024]{0,1:T(8,128)} %copy-done.1) | copy-start | bytes 25165828
  110.7 9.2 %slice-start = ((s8[8388608]{0:T(1024)(128)(4,1)}), s8[4194304]{0:T(1024)(128)(4,1)S(1)}, s32[]{:S(2)}) async-start(s8[8388608]{0:T(1024)(128)(4,1)} %bitcast.3), calls=%async_computation.3 | async-start | bytes 8388608
  110.8 9.2 %copy-start.4 = (bf16[2048,1024]{1,0:T(8,128)(2,1)S(1)}, bf16[2048,1024]{1,0:T(8,128)(2,1)}, u32[]{:S(2)}) copy-start(bf16[2048,1024]{1,0:T(8,128)(2,1)} %param.3) | copy-start | bytes 12582916
  114.9 5.5 %slice-start.1 = ((s8[8388608]{0:T(1024)(128)(4,1)}), s8[4194304]{0:T(1024)(128)(4,1)S(1)}, s32[]{:S(2)}) async-start(s8[8388608]{0:T(1024)(128)(4,1)} %bitcast.3), calls=%async_computation.4 | async-start | bytes 8388608
  126.6 127.6 %all-reduce.2.cloned.1.call-start = ((), (), s32[]{:S(2)}) async-start(), calls=%async_computation.2 | async-start | bytes 2097152 | tf_op jit(solution)/shard_map/psum | solution.py:34
Sparse Core Ops, SparseCore 0:
  126.7 45.1 reduce-scatter.1
  175.8 78.3 all-reduce.1
where the time goes:
time: 264 us; the launch traced here: 263 us
  blocking collectives  122 us (46%)
  waiting for transfers between devices  82.6 us (31%)
  other arithmetic  26 us (10%)
  between operations  14.2 us (5%)
  matrix products  12.5 us (5%)
  local copies, waits for them, and re-layouts  5.75 us (2%)
    psum x3, blocking collectives, per_device(): column_mass = lax.psum(jnp.sum(mass, axis=0), ('rows', 'sub'))  122 us
    reduce_scatter x1, waiting for transfers between devices, per_device(): own = lax.psum_scatter(total, 'sub', scatter_dimension=0, tiled=True)  45.3 us
    psum x1, waiting for transfers between devices, per_device(): lax.psum(lax.dot_general(plan, documents, (((0,), (0,)), ((), ())), prefe...  37.3 us
    reduce_max x2, other arithmetic, per_device(): lse = jax.nn.logsumexp(scores + duals[None, :], axis=1)  8.3 us
    reduce_sum x3, other arithmetic, per_device(): lse = jax.nn.logsumexp(scores + duals[None, :], axis=1)  7.93 us
    reduce_sum x3, other arithmetic, per_device(): column_mass = lax.psum(jnp.sum(mass, axis=0), ('rows', 'sub'))  6.95 us
    dot_general x1, matrix products, per_device(): lax.dot_general(documents, centroids, (((1,), (1,)), ((), ())), preferred...  6.38 us
    dot_general x1, matrix products, per_device(): lax.dot_general(plan, documents, (((0,), (0,)), ((), ())), preferred_elem...  6.12 us
  transfers between devices with their start and end apart: 2, of which 2 were waited for; matrix products, arithmetic and copies ran while one was open for 2% of the time, Pallas kernels for 0%

commit v1 on v0

v1 whole, which is shorter than its diff:
```python
import functools
import math

import jax
import jax.numpy as jnp
from jax import lax
from jax.experimental import pallas as pl
from jax.experimental.pallas import tpu as pltpu
from jax.sharding import PartitionSpec as P

ITERS = 3
TAU = 0.8
TEMP = 4.0
LANES = 128
TILE = 256
F32, BF16 = jnp.float32, jnp.bfloat16
MESH = pl.DeviceIdType.MESH


def kernel(n_rows, n_sub, docs_hbm, cent_hbm, cmass_ref, out_hbm, duals_ref,
           docs, cent, scores, plan, dual_b, acc, col, p1, p2, core_s, core_r, own, y_s, y_r, r_s, r_r, gath,
           in_sem, out_sem, p1_ss, p1_rs, p2_ss, p2_rs, c_ss, c_rs, y_ss, y_rs, r_ss, r_rs, gz_ss, gz_rs, gx_ss, gx_rs):
    n_docs, d = docs.shape
    k_all = cent.shape[0]
    slab = k_all // n_sub
    rps = slab // LANES
    h, w = own.shape[1:]
    nbh = slab // h
    n_ct = d // TILE
    bpc = n_rows // n_ct
    r, s = lax.axis_index("rows"), lax.axis_index("sub")
    s1 = s + 1 - 2 * lax.rem(s, 2)
    s2 = lax.rem(s + 2, n_sub)
    s3 = n_sub - 1 - s
    order = (s3, s1, s2, s)
    r1 = r + 1 - 2 * lax.rem(r, 2)

    barrier = pltpu.get_barrier_semaphore()
    for t in (s1, s2, s3):
        pl.semaphore_signal(barrier, inc=1, device_id=(r, t), device_id_type=MESH)

    def greet(i, _):
        pl.semaphore_signal(barrier, inc=1, device_id=(lax.rem(r + i, n_rows), s), device_id_type=MESH)
        return 0

    lax.fori_loop(1, n_rows, greet, 0)

    def cent_copy(l):
        rows = pl.ds(pl.multiple_of(order[l] * slab, slab), slab)
        return pltpu.make_async_copy(cent_hbm.at[rows, :], cent.at[pl.ds(l * slab, slab), :], in_sem.at[l])

    def docs_copy(c):
        rows = pl.ds(pl.multiple_of(c * TILE, TILE), TILE)
        return pltpu.make_async_copy(docs_hbm.at[rows, :], docs.at[rows, :], in_sem.at[n_sub + c])

    n_chunks = n_docs // TILE
    docs_copy(0).start()
    for l in range(n_sub):
        cent_copy(l).start()
    for c in range(1, n_chunks):
        docs_copy(c).start()
    for l in range(n_sub):
        cent_copy(l).wait()

    scale = TEMP / math.sqrt(d)
    loga = -math.log(n_docs * n_rows * n_sub)

    def fold(read, op, axis_op):
        size = k_all // 8
        parts = [axis_op(read(pl.ds(q * size, size)).reshape(size // 8, 8, LANES), axis=0) for q in range(8)]
        while len(parts) > 1:
            parts = [op(a, b) for a, b in zip(parts[::2], parts[1::2])]
        return axis_op(parts[0], axis=0, keepdims=True)

    def chunk(it, c):
        for u in range(TILE // LANES):
            cols = pl.ds(pl.multiple_of(c * TILE + u * LANES, LANES), LANES)
            if it == 0:
                read = lambda ks: scores[ks, cols]
            else:
                read = lambda ks: scores[ks, cols] + dual_b[ks, :]
            top = fold(read, jnp.maximum, jnp.max)
            total = fold(lambda ks: jnp.exp(read(ks) - top), jnp.add, jnp.sum)
            row_dual = TAU * (loga - (top + jnp.log(total)))
            mass = jnp.exp(scores[:, cols] + row_dual)
            acc[...] += mass
            if it == ITERS - 1:
                plan[:, cols] = mass.astype(BF16)

    def first(c, _):
        docs_copy(c).wait()
        rows = pl.ds(pl.multiple_of(c * TILE, TILE), TILE)
        scores[:, rows] = lax.dot_general(
            cent[...], docs[rows, :], (((1,), (1,)), ((), ())), preferred_element_type=F32
        ) * scale
        chunk(0, c)
        return 0

    def later(it, c, _):
        chunk(it, c)
        return 0

    def p1_copy(it, i):
        t = (s1, s2, s3)[i]
        return pltpu.make_async_remote_copy(
            p1.at[it, s], p1.at[it, s], p1_ss.at[it, i], p1_rs.at[it, i], device_id=(r, t), device_id_type=MESH
        )

    def p1_arrival(it, i):
        t = (s1, s2, s3)[i]
        return pltpu.make_async_remote_copy(
            p1.at[it, t], p1.at[it, t], p1_ss.at[it, i], p1_rs.at[it, i], device_id=(r, t), device_id_type=MESH
        )

    def p2_copy(it, i):
        t = lax.rem(r + i, n_rows)
        return pltpu.make_async_remote_copy(
            p2.at[it, r], p2.at[it, r], p2_ss.at[it, i], p2_rs.at[it, i], device_id=(t, s), device_id_type=MESH
        )

    def p2_arrival(it, i):
        t = lax.rem(r - i + n_rows, n_rows)
        return pltpu.make_async_remote_copy(
            p2.at[it, t], p2.at[it, t], p2_ss.at[it, i], p2_rs.at[it, i], device_id=(t, s), device_id_type=MESH
        )

    def over(start, n, f):
        def body(i, _):
            f(i)
            return 0
        lax.fori_loop(start, n, body, 0)

    def mass_send(it):
        for l in range(n_sub):
            for j in range(rps):
                block = acc[pl.ds(l * slab + j * LANES, LANES), :]
                p1[it, s, pl.ds(order[l] * rps + j, 1), :] = jnp.sum(block.T, axis=0, keepdims=True)
        for i in range(3):
            p1_copy(it, i).start()

    def mass_mid(it):
        for i in range(3):
            p1_arrival(it, i).wait_recv()
        p2[it, r] = (p1[it, 0] + p1[it, 1]) + (p1[it, 2] + p1[it, 3])
        over(1, n_rows, lambda i: p2_copy(it, i).start())

    def spread(value_ref, first_slab):
        for l in range(first_slab, n_sub):
            for j in range(rps):
                row = value_ref[pl.ds(order[l] * rps + j, 1), :]
                dual_b[pl.ds(l * slab + j * LANES, LANES), :] = jnp.broadcast_to(row, (LANES, LANES)).T

    def mass_end(it):
        over(1, n_rows, lambda i: p2_arrival(it, i).wait_recv())
        col[...] = lax.fori_loop(1, n_rows, lambda i, a: a + p2[it, i], p2[it, 0])
        duals_ref[...] = TAU * (jnp.log(cmass_ref[...]) - jnp.log(col[...]))
        if it < ITERS - 1:
            spread(duals_ref, 0)
        else:
            spread(col, n_sub - 1)
        for i in range(3):
            p1_copy(it, i).wait_send()
        over(1, n_rows, lambda i: p2_copy(it, i).wait_send())

    for it in range(ITERS):
        acc[...] = jnp.zeros_like(acc)
        lax.fori_loop(0, n_chunks, first if it == 0 else functools.partial(later, it), 0)
        if it == 0:
            pl.semaphore_wait(barrier, 3 + n_rows - 1)
        mass_send(it)
        if it < ITERS - 1:
            mass_mid(it)
            mass_end(it)

    tiles = [lax.rem(lax.div(r, bpc) + 1 + j, n_ct) for j in range(n_ct)]

    def product(first_row, j):
        cols = pl.ds(pl.multiple_of(tiles[j] * TILE, TILE), TILE)
        return jnp.dot(plan[pl.ds(first_row, 2 * slab), :], docs[:, cols], preferred_element_type=F32)

    def core_copy(j):
        return pltpu.make_async_remote_copy(
            core_s.at[j], core_r.at[j], c_ss.at[j], c_rs.at[j], device_id=(r, s1), device_id_type=MESH
        )

    def y_copy(m):
        return pltpu.make_async_remote_copy(
            y_s.at[m], y_r.at[m], y_ss.at[m], y_rs.at[m], device_id=(r, s2), device_id_type=MESH
        )

    def far(j):
        core_s[j] = product(0, j)
        core_copy(j).start()

    def near(j):
        both = product(2 * slab, j)
        core_copy(j).wait_recv()
        both = both + core_r[j]
        for q in range(bpc):
            m, i, c = j * bpc + q, (q % nbh) * h, (q // nbh) * w
            y_s[m] = both[i:i + h, c:c + w].astype(BF16)
            y_copy(m).start()
            own[m] = both[slab + i:slab + i + h, c:c + w]

    far(0)
    far(1)
    mass_mid(ITERS - 1)
    near(0)
    for j in range(1, n_ct):
        if j + 1 < n_ct:
            far(j + 1)
        near(j)

    def block_of(m):
        return tiles[m // bpc] * bpc + m % bpc

    def r_copy(m):
        b = block_of(m)
        return pltpu.make_async_remote_copy(
            r_s.at[m], r_r.at[r], r_ss.at[m], r_rs.at[r], device_id=(b, s), device_id_type=MESH
        )

    def r_arrival(t):
        return pltpu.make_async_remote_copy(
            r_r.at[t], r_r.at[t], r_ss.at[0], r_rs.at[t], device_id=(t, s), device_id_type=MESH
        )

    for m in range(n_rows):
        y_copy(m).wait_recv()
        value = own[m] + y_r[m].astype(F32)
        if m < n_rows - bpc:
            r_s[m] = value.astype(BF16)
            r_copy(m).start()
        else:
            own[m] = value

            @pl.when(block_of(m) != r)
            def _():
                r_s[m] = own[m].astype(BF16)
                r_copy(m).start()

    mass_end(ITERS - 1)

    mine = own[n_rows - bpc + lax.rem(r, bpc)]

    def gather_sum(i, total):
        t = lax.rem(r - i + n_rows, n_rows)
        r_arrival(t).wait_recv()
        return total + r_r[t].astype(F32)

    total = lax.fori_loop(1, n_rows, gather_sum, mine)
    i0 = pl.multiple_of((n_sub - 1) * slab + lax.rem(r, nbh) * h, h)
    gath[r] = (total / dual_b[pl.ds(i0, h), :]).astype(BF16)

    half = n_rows // 2

    def z_copy(i):
        return pltpu.make_async_remote_copy(
            gath.at[r], gath.at[r], gz_ss.at[i], gz_rs.at[i],
            device_id=(lax.rem(r + 2 * i, n_rows), s), device_id_type=MESH,
        )

    def z_arrival(i):
        t = lax.rem(r - 2 * i + n_rows, n_rows)
        return pltpu.make_async_remote_copy(
            gath.at[t], gath.at[t], gz_ss.at[i], gz_rs.at[i], device_id=(t, s), device_id_type=MESH
        )

    def x_copy(i):
        t = lax.rem(r - 2 * i + n_rows, n_rows)
        return pltpu.make_async_remote_copy(
            gath.at[t], gath.at[t], gx_ss.at[i], gx_rs.at[i], device_id=(r1, s), device_id_type=MESH
        )

    def x_arrival(i):
        t = lax.rem(r1 - 2 * i + n_rows, n_rows)
        return pltpu.make_async_remote_copy(
            gath.at[t], gath.at[t], gx_ss.at[i], gx_rs.at[i], device_id=(r1, s), device_id_type=MESH
        )

    def store(b, i):
        rows = pl.ds(pl.multiple_of(lax.rem(b, nbh) * h, h), h)
        cols = pl.ds(pl.multiple_of(lax.div(b, nbh) * w, w), w)
        return pltpu.make_async_copy(gath.at[b], out_hbm.at[rows, cols], out_sem.at[i])

    over(1, half, lambda i: z_copy(i).start())
    x_copy(0).start()
    store(r, 0).start()

    def forward(i):
        z_arrival(i).wait_recv()
        x_copy(i).start()
        store(lax.rem(r - 2 * i + n_rows, n_rows), i).start()

    over(1, half, forward)

    def keep(i):
        x_arrival(i).wait_recv()
        store(lax.rem(r1 - 2 * i + n_rows, n_rows), half + i).start()

    over(0, half, keep)

    for j in range(n_ct):
        core_copy(j).wait_send()
    over(0, n_rows, lambda m: y_copy(m).wait_send())
    for m in range(n_rows):
        if m < n_rows - bpc:
            r_copy(m).wait_send()
        else:
            @pl.when(block_of(m) != r)
            def _():
                r_copy(m).wait_send()
    over(1, half, lambda i: z_copy(i).wait_send())
    over(0, half, lambda i: x_copy(i).wait_send())
    over(0, half, lambda i: store(lax.rem(r - 2 * i + n_rows, n_rows), i).wait())
    over(0, half, lambda i: store(lax.rem(r1 - 2 * i + n_rows, n_rows), half + i).wait())


def per_device(n_rows, n_sub, documents, centroids, cluster_mass):
    n_docs, d = documents.shape
    k = centroids.shape[0]
    slab = k // n_sub
    n_ct = d // TILE
    w = LANES
    h = slab * d // (w * n_rows)
    dma = pltpu.SemaphoreType.DMA
    vm = pltpu.VMEM
    blocks = (n_rows, h, w)
    out, duals = pl.pallas_call(
        functools.partial(kernel, n_rows, n_sub),
        out_shape=(
            jax.ShapeDtypeStruct((slab, d), BF16),
            jax.ShapeDtypeStruct((k // LANES, LANES), F32),
        ),
        in_specs=[
            pl.BlockSpec(memory_space=pl.ANY),
            pl.BlockSpec(memory_space=pl.ANY),
            pl.BlockSpec(memory_space=pltpu.VMEM),
        ],
        out_specs=(pl.BlockSpec(memory_space=pl.ANY), pl.BlockSpec(memory_space=pltpu.VMEM)),
        scratch_shapes=[
            vm((n_docs, d), BF16), vm((k, d), BF16), vm((k, n_docs), F32), vm((k, n_docs), BF16),
            vm((k, LANES), F32), vm((k, LANES), F32), vm((k // LANES, LANES), F32),
            vm((ITERS, n_sub, k // LANES, LANES), F32), vm((ITERS, n_rows, k // LANES, LANES), F32),
            vm((n_ct, 2 * slab, TILE), F32), vm((n_ct, 2 * slab, TILE), F32),
            vm(blocks, F32), vm(blocks, BF16), vm(blocks, BF16), vm(blocks, BF16), vm(blocks, BF16), vm(blocks, BF16),
            dma((n_sub + n_docs // TILE,)), dma((n_rows,)),
            dma((ITERS, 3)), dma((ITERS, 3)), dma((ITERS, n_rows)), dma((ITERS, n_rows)),
            dma((n_ct,)), dma((n_ct,)), dma((n_rows,)), dma((n_rows,)), dma((n_rows,)), dma((n_rows,)),
            dma((n_rows // 2,)), dma((n_rows // 2,)), dma((n_rows // 2,)), dma((n_rows // 2,)),
        ],
        compiler_params=pltpu.CompilerParams(
            collective_id=0, has_side_effects=True, vmem_limit_bytes=48 * 1024 * 1024
        ),
        cost_estimate=pl.CostEstimate(
            flops=4 * n_docs * k * d, bytes_accessed=2 * (n_docs * d + k * d + slab * d),
            transcendentals=2 * ITERS * n_docs * k,
        ),
    )(documents, centroids, cluster_mass.reshape(k // LANES, LANES))
    return out, duals.reshape(k)


def solution(mesh):
    return jax.shard_map(
        functools.partial(per_device, mesh.shape["rows"], mesh.shape["sub"]),
        mesh=mesh,
        in_specs=(P(("rows", "sub"), None), P(), P()),
        out_specs=(P("sub", None), P()),
        check_vma=False,
    )
```

time: 264 us -> 80.6 us (0.31)
  blocking collectives: 122 us -> 0 us
  waiting for transfers between devices: 82.6 us -> 0 us
  Pallas kernels: 0 us -> 76.1 us
  other arithmetic: 26 us -> 0 us
  between operations: 14.2 us -> 0.65 us
  matrix products: 12.5 us -> 0 us
    psum x3 -> x0, blocking collectives: 122 us -> none  [per_device(): column_mass = lax.psum(jnp.sum(mass, axis=0), ('rows', 'sub'))]
    pallas_call x0 -> x1, Pallas kernels: none -> 76.1 us  [per_device(): pl.pallas_call(functools.partial(kernel, n_rows, n_sub), out_shape=(jax.S...]
    reduce_scatter x1 -> x0, waiting for transfers between devices: 45.3 us -> none  [per_device(): own = lax.psum_scatter(total, 'sub', scatter_dimension=0, tiled=True)]
    psum x1 -> x0, waiting for transfers between devices: 37.3 us -> none  [per_device(): lax.psum(lax.dot_general(plan, documents, (((0,), (0,)), ((), ())), prefe...]
    reduce_sum x6 -> x0, other arithmetic: 14.9 us -> none  [the longest x3 7.93 us: per_device(): lse = jax.nn.logsumexp(scores + duals[None, :], axis=1)]
    dot_general x2 -> x0, matrix products: 12.5 us -> none  [the longest x1 6.38 us: per_device(): lax.dot_general(documents, centroids, (((1,), (1,)), ((), ())), preferred...]
    reduce_max x2 -> x0, other arithmetic: 8.3 us -> none  [per_device(): lse = jax.nn.logsumexp(scores + duals[None, :], axis=1)]
    unnamed x14 -> x6, local copies, waits for them, and re-layouts: 5.68 us -> 3.66 us
  transfers between devices with their start and end apart: 2 -> 0, of which waited for: 2 -> 0; matrix products, arithmetic and copies ran while one was open for 2% -> 0% of each run, Pallas kernels for 0% -> 0%
where the time goes in v1:
time: 80.6 us; the launch traced here: 80.5 us
  Pallas kernels  76.1 us (94%)
  local copies, waits for them, and re-layouts  3.66 us (5%)
    pallas_call x1, Pallas kernels, per_device(): pl.pallas_call(functools.partial(kernel, n_rows, n_sub), out_shape=(jax.S...  76.1 us
    unnamed x6, local copies, waits for them, and re-layouts  3.66 us

profile of v1, /device:TPU:0, one launch (start us, length us, event | category | flops | bytes accessed | tf_op | source)
XLA Modules:
  0.0 80.5 jit_solution(3177240837711813061)
XLA Ops:
  0.6 0.0 copy-start
  0.6 1.6 %copy-done = bf16[1024,1024]{1,0:T(8,128)(2,1)S(1)} copy-done((bf16[1024,1024]{1,0:T(8,128)(2,1)S(1)}, bf16[1024,1024]{1,0:T(8,128)(2,1)}, u32[]{:S(2)}) %copy-start) | copy-done | bytes 2097176
  2.2 0.0 copy-start.1
  2.2 0.7 copy-done.1
  2.9 76.1 %shard_map.50 = (bf16[256,1024]{1,0:T(8,128)(2,1)S(1)}, f32[8,128]{1,0:T(8,128)S(1)}) custom-call(bf16[2048,1024]{1,0:T(8,128)(2,1)} %docs_hbm.1, bf16[1024,1024]{1,0:T(8,128)(2,1)S(1)} %copy-done, f32[8,128]{1,0:T(8,128)S(1)} %bitcast.3), custom_call_target="tpu_custom_call" | custom-call | flops 8589934592 | bytes 6815744 | tf_op jit(solution)/shard_map/pallas_call | solution.py:329
  79.1 0.8 copy.7
  79.9 0.6 copy.8
Async XLA Ops:
  0.6 1.6 %copy-start = (bf16[1024,1024]{1,0:T(8,128)(2,1)S(1)}, bf16[1024,1024]{1,0:T(8,128)(2,1)}, u32[]{:S(2)}) copy-start(bf16[1024,1024]{1,0:T(8,128)(2,1)} %cent_hbm.1) | copy-start | bytes 6291460
  2.2 0.7 copy-start.1

commit v2 on v1

--- a/solution.py
+++ b/solution.py
@@ -11,14 +11,16 @@
 ITERS = 3
 TAU = 0.8
 TEMP = 4.0
+LOG2E = math.log2(math.e)
+HEADROOM = 112.0
 LANES = 128
 TILE = 256
 F32, BF16 = jnp.float32, jnp.bfloat16
 MESH = pl.DeviceIdType.MESH
 
 
-def kernel(n_rows, n_sub, docs_hbm, cent_hbm, cmass_ref, out_hbm, duals_ref,
-           docs, cent, scores, plan, dual_b, acc, col, p1, p2, core_s, core_r, own, y_s, y_r, r_s, r_r, gath,
+def kernel(n_rows, n_sub, docs_hbm, cent_hbm, cmass_hbm, out_hbm, duals_ref,
+           docs, cent, scores, plan, dual_b, acc, col, cmass, shifted, adjust, lse, p1, p2, core_s, core_r, own, y_s, y_r, r_s, r_r, gath,
            in_sem, out_sem, p1_ss, p1_rs, p2_ss, p2_rs, c_ss, c_rs, y_ss, y_rs, r_ss, r_rs, gz_ss, gz_rs, gx_ss, gx_rs):
     n_docs, d = docs.shape
     k_all = cent.shape[0]
@@ -59,46 +61,81 @@
         cent_copy(l).start()
     for c in range(1, n_chunks):
         docs_copy(c).start()
+    cmass_copy = pltpu.make_async_copy(cmass_hbm, cmass, in_sem.at[n_sub + n_chunks])
+    cmass_copy.start()
     for l in range(n_sub):
         cent_copy(l).wait()
-
-    scale = TEMP / math.sqrt(d)
-    loga = -math.log(n_docs * n_rows * n_sub)
-
-    def fold(read, op, axis_op):
-        size = k_all // 8
-        parts = [axis_op(read(pl.ds(q * size, size)).reshape(size // 8, 8, LANES), axis=0) for q in range(8)]
-        while len(parts) > 1:
-            parts = [op(a, b) for a, b in zip(parts[::2], parts[1::2])]
-        return axis_op(parts[0], axis=0, keepdims=True)
-
-    def chunk(it, c):
-        for u in range(TILE // LANES):
-            cols = pl.ds(pl.multiple_of(c * TILE + u * LANES, LANES), LANES)
+    cmass_copy.wait()
+
+    scale = TEMP / math.sqrt(d) * LOG2E
+    loga = -math.log2(n_docs * n_rows * n_sub)
+    parts = 8
+    size = k_all // parts
+    slices = [pl.ds(q * size, size) for q in range(parts)]
+
+    def halves(c):
+        return [pl.ds(pl.multiple_of(c * TILE + u * LANES, LANES), LANES) for u in range(TILE // LANES)]
+
+    def eight(value, axis_op):
+        return axis_op(value.reshape(size // 8, 8, LANES), axis=0)
+
+    def tree(values, op, axis_op):
+        while len(values) > 1:
+            values = [op(a, b) for a, b in zip(values[::2], values[1::2])]
+        return axis_op(values[0], axis=0, keepdims=True)
+
+    def mass_slice(it, ks, cols, row_duals):
+        masses = [jnp.exp2(scores[ks, cu] + rd) for cu, rd in zip(cols, row_duals)]
+        acc[ks, :] += sum(masses[1:], masses[0])
+        if it == ITERS - 1:
+            for cu, mass in zip(cols, masses):
+                plan[ks, cu] = mass.astype(BF16)
+
+    def step(it, following, current, row_duals):
+        sums = None
+        if following is not None:
+            cols = halves(following)
             if it == 0:
-                read = lambda ks: scores[ks, cols]
+                shift = [
+                    tree([eight(scores[ks, cu], jnp.max) for ks in slices], jnp.maximum, jnp.max) for cu in cols
+                ]
             else:
-                read = lambda ks: scores[ks, cols] + dual_b[ks, :]
-            top = fold(read, jnp.maximum, jnp.max)
-            total = fold(lambda ks: jnp.exp(read(ks) - top), jnp.add, jnp.sum)
-            row_dual = TAU * (loga - (top + jnp.log(total)))
-            mass = jnp.exp(scores[:, cols] + row_dual)
-            acc[...] += mass
-            if it == ITERS - 1:
-                plan[:, cols] = mass.astype(BF16)
-
-    def first(c, _):
-        docs_copy(c).wait()
-        rows = pl.ds(pl.multiple_of(c * TILE, TILE), TILE)
-        scores[:, rows] = lax.dot_general(
-            cent[...], docs[rows, :], (((1,), (1,)), ((), ())), preferred_element_type=F32
-        ) * scale
-        chunk(0, c)
-        return 0
-
-    def later(it, c, _):
-        chunk(it, c)
-        return 0
+                shift = [lse[:, cu] for cu in cols]
+            sums = [[] for _ in cols]
+        for ks in slices:
+            if following is not None:
+                for cu, top, out in zip(cols, shift, sums):
+                    x = scores[ks, cu] if it == 0 else scores[ks, cu] + dual_b[ks, :]
+                    out.append(eight(jnp.exp2(x - top), jnp.sum))
+            if current is not None:
+                mass_slice(it, ks, halves(current), row_duals)
+        if following is None:
+            return None
+        result = []
+        for cu, top, values in zip(cols, shift, sums):
+            value = top + jnp.log(tree(values, jnp.add, jnp.sum)) * LOG2E
+            if it > 0:
+                value = value + adjust[...]
+            lse[:, cu] = value
+            result.append(TAU * (loga - value))
+        return tuple(result)
+
+    def first_pass():
+        row_duals = None
+        for c in range(n_chunks + 2):
+            if c < n_chunks:
+                docs_copy(c).wait()
+                rows = pl.ds(c * TILE, TILE)
+                scores[:, rows] = lax.dot_general(
+                    cent[...], docs[rows, :], (((1,), (1,)), ((), ())), preferred_element_type=F32
+                ) * scale
+            if c >= 1:
+                row_duals = step(0, c - 1 if c <= n_chunks else None, c - 2 if c >= 2 else None, row_duals)
+
+    def later_pass(it):
+        row_duals = step(it, 0, None, None)
+        row_duals = lax.fori_loop(0, n_chunks - 1, lambda c, rd: step(it, c + 1, c, rd), row_duals)
+        step(it, None, n_chunks - 1, row_duals)
 
     def p1_copy(it, i):
         t = (s1, s2, s3)[i]
@@ -153,10 +190,16 @@
     def mass_end(it):
         over(1, n_rows, lambda i: p2_arrival(it, i).wait_recv())
         col[...] = lax.fori_loop(1, n_rows, lambda i, a: a + p2[it, i], p2[it, 0])
-        duals_ref[...] = TAU * (jnp.log(cmass_ref[...]) - jnp.log(col[...]))
+        new = TAU * (jnp.log(cmass[...]) - jnp.log(col[...]))
         if it < ITERS - 1:
-            spread(duals_ref, 0)
+            change = LOG2E * (new if it == 0 else new - duals_ref[...])
+            most = jnp.max(jnp.max(change, axis=0, keepdims=True), axis=1, keepdims=True)
+            adjust[...] = jnp.broadcast_to(most - HEADROOM, adjust.shape)
+            shifted[...] = LOG2E * new - (most - HEADROOM)
+            duals_ref[...] = new
+            spread(shifted, 0)
         else:
+            duals_ref[...] = new
             spread(col, n_sub - 1)
         for i in range(3):
             p1_copy(it, i).wait_send()
@@ -164,7 +207,10 @@
 
     for it in range(ITERS):
         acc[...] = jnp.zeros_like(acc)
-        lax.fori_loop(0, n_chunks, first if it == 0 else functools.partial(later, it), 0)
+        if it == 0:
+            first_pass()
+        else:
+            later_pass(it)
         if it == 0:
             pl.semaphore_wait(barrier, 3 + n_rows - 1)
         mass_send(it)
@@ -335,22 +381,23 @@
         in_specs=[
             pl.BlockSpec(memory_space=pl.ANY),
             pl.BlockSpec(memory_space=pl.ANY),
-            pl.BlockSpec(memory_space=pltpu.VMEM),
+            pl.BlockSpec(memory_space=pl.ANY),
         ],
         out_specs=(pl.BlockSpec(memory_space=pl.ANY), pl.BlockSpec(memory_space=pltpu.VMEM)),
         scratch_shapes=[
             vm((n_docs, d), BF16), vm((k, d), BF16), vm((k, n_docs), F32), vm((k, n_docs), BF16),
-            vm((k, LANES), F32), vm((k, LANES), F32), vm((k // LANES, LANES), F32),
+            vm((k, LANES), F32), vm((k, LANES), F32),
+            vm((k // LANES, LANES), F32), vm((k // LANES, LANES), F32), vm((k // LANES, LANES), F32), vm((1, LANES), F32), vm((1, n_docs), F32),
             vm((ITERS, n_sub, k // LANES, LANES), F32), vm((ITERS, n_rows, k // LANES, LANES), F32),
             vm((n_ct, 2 * slab, TILE), F32), vm((n_ct, 2 * slab, TILE), F32),
             vm(blocks, F32), vm(blocks, BF16), vm(blocks, BF16), vm(blocks, BF16), vm(blocks, BF16), vm(blocks, BF16),
-            dma((n_sub + n_docs // TILE,)), dma((n_rows,)),
+            dma((n_sub + n_docs // TILE + 1,)), dma((n_rows,)),
             dma((ITERS, 3)), dma((ITERS, 3)), dma((ITERS, n_rows)), dma((ITERS, n_rows)),
             dma((n_ct,)), dma((n_ct,)), dma((n_rows,)), dma((n_rows,)), dma((n_rows,)), dma((n_rows,)),
             dma((n_rows // 2,)), dma((n_rows // 2,)), dma((n_rows // 2,)), dma((n_rows // 2,)),
         ],
         compiler_params=pltpu.CompilerParams(
-            collective_id=0, has_side_effects=True, vmem_limit_bytes=48 * 1024 * 1024
+            collective_id=0, has_side_effects=True, vmem_limit_bytes=60 * 1024 * 1024
         ),
         cost_estimate=pl.CostEstimate(
             flops=4 * n_docs * k * d, bytes_accessed=2 * (n_docs * d + k * d + slab * d),

time: 80.6 us -> 81.6 us (1.012)
  Pallas kernels: 76.1 us -> 77.7 us
    pallas_call x1, Pallas kernels: 76.1 us -> 77.7 us  [per_device(): pl.pallas_call(functools.partial(kernel, n_rows, n_sub), out_shape=(jax.S...]
    unnamed x6 -> x2, local copies, waits for them, and re-layouts: 3.66 us -> 3.13 us
where the time goes in v2:
time: 81.6 us; the launch traced here: 81.4 us
  Pallas kernels  77.7 us (95%)
  local copies, waits for them, and re-layouts  3.13 us (4%)
    pallas_call x1, Pallas kernels, per_device(): pl.pallas_call(functools.partial(kernel, n_rows, n_sub), out_shape=(jax.S...  77.7 us
    unnamed x2, local copies, waits for them, and re-layouts  3.13 us

profile of v2, /device:TPU:0, one launch (start us, length us, event | category | flops | bytes accessed | tf_op | source)
XLA Modules:
  0.0 81.4 jit_solution(8799854439041131916)
XLA Ops:
  0.6 77.7 %shard_map.50 = (bf16[256,1024]{1,0:T(8,128)(2,1)}, f32[8,128]{1,0:T(8,128)}) custom-call(bf16[2048,1024]{1,0:T(8,128)(2,1)} %docs_hbm.1, bf16[1024,1024]{1,0:T(8,128)(2,1)} %cent_hbm.1, f32[8,128]{1,0:T(8,128)} %bitcast.3), custom_call_target="tpu_custom_call" | custom-call | flops 8589934592 | bytes 6815744 | tf_op jit(solution)/shard_map/pallas_call | solution.py:375
  78.3 1.9 %copy.7 = bf16[256,1024]{1,0:T(8,128)(2,1)} copy(bf16[256,1024]{1,0:T(8,128)(2,1)} %get-tuple-element.8) | data formatting | bytes 1048576
  80.2 1.3 %copy.8 = f32[1024]{0:T(1024)} copy(f32[1024]{0:T(1024)} %bitcast.2) | data formatting | bytes 8192

commit v3 on v2

--- a/solution.py
+++ b/solution.py
@@ -84,18 +84,18 @@
             values = [op(a, b) for a, b in zip(values[::2], values[1::2])]
         return axis_op(values[0], axis=0, keepdims=True)
 
-    def mass_slice(it, ks, cols, row_duals):
+    def mass_slice(keep, ks, cols, row_duals):
         masses = [jnp.exp2(scores[ks, cu] + rd) for cu, rd in zip(cols, row_duals)]
         acc[ks, :] += sum(masses[1:], masses[0])
-        if it == ITERS - 1:
+        if keep:
             for cu, mass in zip(cols, masses):
                 plan[ks, cu] = mass.astype(BF16)
 
-    def step(it, following, current, row_duals):
+    def step(initial, following, current, row_duals):
         sums = None
         if following is not None:
             cols = halves(following)
-            if it == 0:
+            if initial:
                 shift = [
                     tree([eight(scores[ks, cu], jnp.max) for ks in slices], jnp.maximum, jnp.max) for cu in cols
                 ]
@@ -105,37 +105,35 @@
         for ks in slices:
             if following is not None:
                 for cu, top, out in zip(cols, shift, sums):
-                    x = scores[ks, cu] if it == 0 else scores[ks, cu] + dual_b[ks, :]
+                    x = scores[ks, cu] if initial else scores[ks, cu] + dual_b[ks, :]
                     out.append(eight(jnp.exp2(x - top), jnp.sum))
             if current is not None:
-                mass_slice(it, ks, halves(current), row_duals)
+                mass_slice(True, ks, halves(current), row_duals)
         if following is None:
             return None
         result = []
         for cu, top, values in zip(cols, shift, sums):
             value = top + jnp.log(tree(values, jnp.add, jnp.sum)) * LOG2E
-            if it > 0:
+            if not initial:
                 value = value + adjust[...]
             lse[:, cu] = value
             result.append(TAU * (loga - value))
         return tuple(result)
 
-    def first_pass():
-        row_duals = None
-        for c in range(n_chunks + 2):
-            if c < n_chunks:
-                docs_copy(c).wait()
-                rows = pl.ds(c * TILE, TILE)
-                scores[:, rows] = lax.dot_general(
-                    cent[...], docs[rows, :], (((1,), (1,)), ((), ())), preferred_element_type=F32
-                ) * scale
-            if c >= 1:
-                row_duals = step(0, c - 1 if c <= n_chunks else None, c - 2 if c >= 2 else None, row_duals)
-
-    def later_pass(it):
-        row_duals = step(it, 0, None, None)
-        row_duals = lax.fori_loop(0, n_chunks - 1, lambda c, rd: step(it, c + 1, c, rd), row_duals)
-        step(it, None, n_chunks - 1, row_duals)
+    def first_chunk(c):
+        docs_copy(c).wait()
+        rows = pl.ds(pl.multiple_of(c * TILE, TILE), TILE)
+        scores[:, rows] = lax.dot_general(
+            cent[...], docs[rows, :], (((1,), (1,)), ((), ())), preferred_element_type=F32
+        ) * scale
+        row_duals = step(True, c, None, None)
+        for ks in slices:
+            mass_slice(False, ks, halves(c), row_duals)
+
+    def later_pass():
+        row_duals = step(False, 0, None, None)
+        row_duals = lax.fori_loop(0, n_chunks - 1, lambda c, rd: step(False, c + 1, c, rd), row_duals)
+        step(False, None, n_chunks - 1, row_duals)
 
     def p1_copy(it, i):
         t = (s1, s2, s3)[i]
@@ -187,41 +185,43 @@
                 row = value_ref[pl.ds(order[l] * rps + j, 1), :]
                 dual_b[pl.ds(l * slab + j * LANES, LANES), :] = jnp.broadcast_to(row, (LANES, LANES)).T
 
-    def mass_end(it):
+    def mass_end(it, last):
         over(1, n_rows, lambda i: p2_arrival(it, i).wait_recv())
         col[...] = lax.fori_loop(1, n_rows, lambda i, a: a + p2[it, i], p2[it, 0])
         new = TAU * (jnp.log(cmass[...]) - jnp.log(col[...]))
-        if it < ITERS - 1:
-            change = LOG2E * (new if it == 0 else new - duals_ref[...])
+        if last:
+            spread(col, n_sub - 1)
+        else:
+            change = LOG2E * (new - duals_ref[...])
             most = jnp.max(jnp.max(change, axis=0, keepdims=True), axis=1, keepdims=True)
             adjust[...] = jnp.broadcast_to(most - HEADROOM, adjust.shape)
             shifted[...] = LOG2E * new - (most - HEADROOM)
-            duals_ref[...] = new
             spread(shifted, 0)
-        else:
-            duals_ref[...] = new
-            spread(col, n_sub - 1)
+        duals_ref[...] = new
         for i in range(3):
             p1_copy(it, i).wait_send()
         over(1, n_rows, lambda i: p2_copy(it, i).wait_send())
 
-    for it in range(ITERS):
+    acc[...] = jnp.zeros_like(acc)
+    duals_ref[...] = jnp.zeros_like(duals_ref)
+    over(0, n_chunks, first_chunk)
+    pl.semaphore_wait(barrier, 3 + n_rows - 1)
+    mass_send(0)
+
+    def iteration(it):
+        mass_mid(it - 1)
+        mass_end(it - 1, False)
         acc[...] = jnp.zeros_like(acc)
-        if it == 0:
-            first_pass()
-        else:
-            later_pass(it)
-        if it == 0:
-            pl.semaphore_wait(barrier, 3 + n_rows - 1)
+        later_pass()
         mass_send(it)
-        if it < ITERS - 1:
-            mass_mid(it)
-            mass_end(it)
-
-    tiles = [lax.rem(lax.div(r, bpc) + 1 + j, n_ct) for j in range(n_ct)]
+
+    over(1, ITERS, iteration)
+
+    def tile_of(j):
+        return lax.rem(lax.div(r, bpc) + 1 + j, n_ct)
 
     def product(first_row, j):
-        cols = pl.ds(pl.multiple_of(tiles[j] * TILE, TILE), TILE)
+        cols = pl.ds(pl.multiple_of(tile_of(j) * TILE, TILE), TILE)
         return jnp.dot(plan[pl.ds(first_row, 2 * slab), :], docs[:, cols], preferred_element_type=F32)
 
     def core_copy(j):
@@ -248,17 +248,12 @@
             y_copy(m).start()
             own[m] = both[slab + i:slab + i + h, c:c + w]
 
-    far(0)
-    far(1)
+    over(0, n_ct, far)
     mass_mid(ITERS - 1)
-    near(0)
-    for j in range(1, n_ct):
-        if j + 1 < n_ct:
-            far(j + 1)
-        near(j)
+    over(0, n_ct, near)
 
     def block_of(m):
-        return tiles[m // bpc] * bpc + m % bpc
+        return tile_of(lax.div(m, bpc)) * bpc + lax.rem(m, bpc)
 
     def r_copy(m):
         b = block_of(m)
@@ -271,21 +266,17 @@
             r_r.at[t], r_r.at[t], r_ss.at[0], r_rs.at[t], device_id=(t, s), device_id_type=MESH
         )
 
-    for m in range(n_rows):
+    def reduce_block(m):
         y_copy(m).wait_recv()
-        value = own[m] + y_r[m].astype(F32)
-        if m < n_rows - bpc:
-            r_s[m] = value.astype(BF16)
+        own[m] = own[m] + y_r[m].astype(F32)
+
+        @pl.when(block_of(m) != r)
+        def _():
+            r_s[m] = own[m].astype(BF16)
             r_copy(m).start()
-        else:
-            own[m] = value
-
-            @pl.when(block_of(m) != r)
-            def _():
-                r_s[m] = own[m].astype(BF16)
-                r_copy(m).start()
-
-    mass_end(ITERS - 1)
+
+    over(0, n_rows, reduce_block)
+    mass_end(ITERS - 1, True)
 
     mine = own[n_rows - bpc + lax.rem(r, bpc)]
 
@@ -346,16 +337,15 @@
 
     over(0, half, keep)
 
-    for j in range(n_ct):
-        core_copy(j).wait_send()
+    over(0, n_ct, lambda j: core_copy(j).wait_send())
     over(0, n_rows, lambda m: y_copy(m).wait_send())
-    for m in range(n_rows):
-        if m < n_rows - bpc:
+
+    def sent(m):
+        @pl.when(block_of(m) != r)
+        def _():
             r_copy(m).wait_send()
-        else:
-            @pl.when(block_of(m) != r)
-            def _():
-                r_copy(m).wait_send()
+
+    over(0, n_rows, sent)
     over(1, half, lambda i: z_copy(i).wait_send())
     over(0, half, lambda i: x_copy(i).wait_send())
     over(0, half, lambda i: store(lax.rem(r - 2 * i + n_rows, n_rows), i).wait())
@@ -397,7 +387,7 @@
             dma((n_rows // 2,)), dma((n_rows // 2,)), dma((n_rows // 2,)), dma((n_rows // 2,)),
         ],
         compiler_params=pltpu.CompilerParams(
-            collective_id=0, has_side_effects=True, vmem_limit_bytes=60 * 1024 * 1024
+            collective_id=0, has_side_effects=True, vmem_limit_bytes=52 * 1024 * 1024
         ),
         cost_estimate=pl.CostEstimate(
             flops=4 * n_docs * k * d, bytes_accessed=2 * (n_docs * d + k * d + slab * d),

time: 81.6 us -> 71.9 us (0.88)
  Pallas kernels: 77.7 us -> 69 us
  local copies, waits for them, and re-layouts: 3.13 us -> 2.07 us
    pallas_call x1, Pallas kernels: 77.7 us -> 69 us  [per_device(): pl.pallas_call(functools.partial(kernel, n_rows, n_sub), out_shape=(jax.S...]
    unnamed x2 -> x4, local copies, waits for them, and re-layouts: 3.13 us -> 2.07 us
where the time goes in v3:
time: 71.9 us; the launch traced here: 71.7 us
  Pallas kernels  69 us (96%)
  local copies, waits for them, and re-layouts  2.07 us (3%)
    pallas_call x1, Pallas kernels, per_device(): pl.pallas_call(functools.partial(kernel, n_rows, n_sub), out_shape=(jax.S...  69 us
    unnamed x4, local copies, waits for them, and re-layouts  2.07 us

profile of v3, /device:TPU:0, one launch (start us, length us, event | category | flops | bytes accessed | tf_op | source)
XLA Modules:
  0.0 71.7 jit_solution(690455277069665694)
XLA Ops:
  0.6 0.0 copy-start
  0.6 0.7 copy-done
  1.3 69.0 %shard_map.50 = (bf16[256,1024]{1,0:T(8,128)(2,1)S(1)}, f32[8,128]{1,0:T(8,128)S(1)}) custom-call(bf16[2048,1024]{1,0:T(8,128)(2,1)} %docs_hbm.1, bf16[1024,1024]{1,0:T(8,128)(2,1)} %cent_hbm.1, f32[8,128]{1,0:T(8,128)S(1)} %bitcast.3), custom_call_target="tpu_custom_call" | custom-call | flops 8589934592 | bytes 6815744 | tf_op jit(solution)/shard_map/pallas_call | solution.py:365
  70.3 0.8 %copy.7 = bf16[256,1024]{1,0:T(8,128)(2,1)} copy(bf16[256,1024]{1,0:T(8,128)(2,1)S(1)} %get-tuple-element.8) | data formatting | bytes 1048576
  71.1 0.6 copy.8
Async XLA Ops:
  0.6 0.7 copy-start

commit v4 on v3

--- a/solution.py
+++ b/solution.py
@@ -20,8 +20,8 @@
 
 
 def kernel(n_rows, n_sub, docs_hbm, cent_hbm, cmass_hbm, out_hbm, duals_ref,
-           docs, cent, scores, plan, dual_b, acc, col, cmass, shifted, adjust, lse, p1, p2, core_s, core_r, own, y_s, y_r, r_s, r_r, gath,
-           in_sem, out_sem, p1_ss, p1_rs, p2_ss, p2_rs, c_ss, c_rs, y_ss, y_rs, r_ss, r_rs, gz_ss, gz_rs, gx_ss, gx_rs):
+           docs, cent, scores, plan, dual_b, acc, col, cmass, shifted, adjust, lse, p1, p2, core_s, core_r, own, away, e_s, e_r, y_s, y_r, r_s, r_r, gath,
+           in_sem, out_sem, p1_ss, p1_rs, p2_ss, p2_rs, c_ss, c_rs, e_ss, e_rs, y_ss, y_rs, r_ss, r_rs, gz_ss, gz_rs, gx_ss, gx_rs):
     n_docs, d = docs.shape
     k_all = cent.shape[0]
     slab = k_all // n_sub
@@ -244,13 +244,53 @@
         both = both + core_r[j]
         for q in range(bpc):
             m, i, c = j * bpc + q, (q % nbh) * h, (q // nbh) * w
-            y_s[m] = both[i:i + h, c:c + w].astype(BF16)
-            y_copy(m).start()
+            away[m] = both[i:i + h, c:c + w]
             own[m] = both[slab + i:slab + i + h, c:c + w]
+
+        @pl.when(j < n_ct // 2)
+        def _():
+            def pair(p):
+                m = j * bpc + 2 * p + 1 - lax.rem(r, 2)
+                e_s[m, 0] = away[m].astype(BF16)
+                e_s[m, 1] = own[m].astype(BF16)
+                e_copy(m).start()
+            over(0, bpc // 2, pair)
+
+        @pl.when(j >= n_ct // 2)
+        def _():
+            over(j * bpc, (j + 1) * bpc, y_send)
+
+    def e_copy(m):
+        return pltpu.make_async_remote_copy(
+            e_s.at[m], e_r.at[m], e_ss.at[m], e_rs.at[m], device_id=(r1, s), device_id_type=MESH
+        )
+
+    def y_send(m):
+        y_s[m] = away[m].astype(BF16)
+        y_copy(m).start()
+
+    early = n_rows // 2
+    pairs = early // 2
+
+    def mine_of(p):
+        return 2 * p + lax.rem(r, 2)
+
+    def theirs_of(p):
+        return 2 * p + 1 - lax.rem(r, 2)
+
+    def e_reduce(p):
+        m = mine_of(p)
+        pltpu.make_async_remote_copy(
+            e_r.at[m], e_r.at[m], e_ss.at[m], e_rs.at[m], device_id=(r1, s), device_id_type=MESH
+        ).wait_recv()
+        away[m] = away[m] + e_r[m, 0].astype(F32)
+        own[m] = own[m] + e_r[m, 1].astype(F32)
+        y_send(m)
 
     over(0, n_ct, far)
     mass_mid(ITERS - 1)
     over(0, n_ct, near)
+    over(0, pairs, e_reduce)
 
     def block_of(m):
         return tile_of(lax.div(m, bpc)) * bpc + lax.rem(m, bpc)
@@ -275,17 +315,25 @@
             r_s[m] = own[m].astype(BF16)
             r_copy(m).start()
 
-    over(0, n_rows, reduce_block)
+    over(0, pairs, lambda p: reduce_block(mine_of(p)))
+    over(early, n_rows, reduce_block)
     mass_end(ITERS - 1, True)
 
-    mine = own[n_rows - bpc + lax.rem(r, bpc)]
-
-    def gather_sum(i, total):
+    final = n_rows - bpc + lax.rem(r, bpc)
+
+    def gather_sum(i, _):
         t = lax.rem(r - i + n_rows, n_rows)
-        r_arrival(t).wait_recv()
-        return total + r_r[t].astype(F32)
-
-    total = lax.fori_loop(1, n_rows, gather_sum, mine)
+        place = lax.rem(lax.div(r, bpc) - lax.div(t, bpc) - 1 + 2 * n_ct, n_ct)
+        expected = lax.rem(lax.rem(i, 2) * (1 - lax.div(2 * place, n_ct)), 2) == 0
+
+        @pl.when(expected)
+        def _():
+            r_arrival(t).wait_recv()
+            own[final] = own[final] + r_r[t].astype(F32)
+        return 0
+
+    lax.fori_loop(1, n_rows, gather_sum, 0)
+    total = own[final]
     i0 = pl.multiple_of((n_sub - 1) * slab + lax.rem(r, nbh) * h, h)
     gath[r] = (total / dual_b[pl.ds(i0, h), :]).astype(BF16)
 
@@ -338,14 +386,17 @@
     over(0, half, keep)
 
     over(0, n_ct, lambda j: core_copy(j).wait_send())
-    over(0, n_rows, lambda m: y_copy(m).wait_send())
+    over(0, pairs, lambda p: e_copy(theirs_of(p)).wait_send())
+    over(0, pairs, lambda p: y_copy(mine_of(p)).wait_send())
+    over(early, n_rows, lambda m: y_copy(m).wait_send())
 
     def sent(m):
         @pl.when(block_of(m) != r)
         def _():
             r_copy(m).wait_send()
 
-    over(0, n_rows, sent)
+    over(0, pairs, lambda p: sent(mine_of(p)))
+    over(early, n_rows, sent)
     over(1, half, lambda i: z_copy(i).wait_send())
     over(0, half, lambda i: x_copy(i).wait_send())
     over(0, half, lambda i: store(lax.rem(r - 2 * i + n_rows, n_rows), i).wait())
@@ -380,10 +431,11 @@
             vm((k // LANES, LANES), F32), vm((k // LANES, LANES), F32), vm((k // LANES, LANES), F32), vm((1, LANES), F32), vm((1, n_docs), F32),
             vm((ITERS, n_sub, k // LANES, LANES), F32), vm((ITERS, n_rows, k // LANES, LANES), F32),
             vm((n_ct, 2 * slab, TILE), F32), vm((n_ct, 2 * slab, TILE), F32),
-            vm(blocks, F32), vm(blocks, BF16), vm(blocks, BF16), vm(blocks, BF16), vm(blocks, BF16), vm(blocks, BF16),
+            vm(blocks, F32), vm(blocks, F32), vm((n_rows // 2, 2, h, w), BF16), vm((n_rows // 2, 2, h, w), BF16),
+            vm(blocks, BF16), vm(blocks, BF16), vm(blocks, BF16), vm(blocks, BF16), vm(blocks, BF16),
             dma((n_sub + n_docs // TILE + 1,)), dma((n_rows,)),
             dma((ITERS, 3)), dma((ITERS, 3)), dma((ITERS, n_rows)), dma((ITERS, n_rows)),
-            dma((n_ct,)), dma((n_ct,)), dma((n_rows,)), dma((n_rows,)), dma((n_rows,)), dma((n_rows,)),
+            dma((n_ct,)), dma((n_ct,)), dma((n_rows // 2,)), dma((n_rows // 2,)), dma((n_rows,)), dma((n_rows,)), dma((n_rows,)), dma((n_rows,)),
             dma((n_rows // 2,)), dma((n_rows // 2,)), dma((n_rows // 2,)), dma((n_rows // 2,)),
         ],
         compiler_params=pltpu.CompilerParams(

time: 71.9 us -> 73.5 us (1.022)
  Pallas kernels: 69 us -> 70.7 us
    pallas_call x1, Pallas kernels: 69 us -> 70.7 us  [per_device(): pl.pallas_call(functools.partial(kernel, n_rows, n_sub), out_shape=(jax.S...]
where the time goes in v4:
time: 73.5 us; the launch traced here: 73.4 us
  Pallas kernels  70.7 us (96%)
  local copies, waits for them, and re-layouts  2.07 us (3%)
    pallas_call x1, Pallas kernels, per_device(): pl.pallas_call(functools.partial(kernel, n_rows, n_sub), out_shape=(jax.S...  70.7 us
    unnamed x4, local copies, waits for them, and re-layouts  2.07 us

profile of v4, /device:TPU:0, one launch (start us, length us, event | category | flops | bytes accessed | tf_op | source)
XLA Modules:
  0.0 73.4 jit_solution(18367623576844202616)
XLA Ops:
  0.6 0.0 copy-start
  0.6 0.7 copy-done
  1.3 70.7 %shard_map.50 = (bf16[256,1024]{1,0:T(8,128)(2,1)S(1)}, f32[8,128]{1,0:T(8,128)S(1)}) custom-call(bf16[2048,1024]{1,0:T(8,128)(2,1)} %docs_hbm.1, bf16[1024,1024]{1,0:T(8,128)(2,1)} %cent_hbm.1, f32[8,128]{1,0:T(8,128)S(1)} %bitcast.3), custom_call_target="tpu_custom_call" | custom-call | flops 8589934592 | bytes 6815744 | tf_op jit(solution)/shard_map/pallas_call | solution.py:416
  72.0 0.8 %copy.7 = bf16[256,1024]{1,0:T(8,128)(2,1)} copy(bf16[256,1024]{1,0:T(8,128)(2,1)S(1)} %get-tuple-element.8) | data formatting | bytes 1048576
  72.8 0.6 copy.8
Async XLA Ops:
  0.6 0.7 copy-start
